TPU v7x, 32 devices: a whole 2x2x4 slice. The times are simulated.
32 devices in a mesh: ctx: 16 (over z, y, core), head: 2 (over x).
Axes of the slice: x: 2, y: 2, z: 4, core: 2. Of those that a mesh axis runs over, the one named last changes fastest.
Arguments:
- queries: bfloat16 [2048, 8192], P('ctx', 'head'), may hold values from -5 to 5
- key_rows: bfloat16 [2048, 1024], P('ctx', 'head'), may hold values from -5 to 5
- value_rows: bfloat16 [2048, 1024], P('ctx', 'head'), may hold values from -6 to 6
- query_tangent: bfloat16 [2048, 8192], P('ctx', 'head'), may hold values from -16 to 16
- key_tangent: bfloat16 [2048, 1024], P('ctx', 'head'), may hold values from -3 to 3
- value_tangent: bfloat16 [2048, 1024], P('ctx', 'head'), may hold values from -6 to 6
- block_order: int32 [16], replicated, may hold values from 0 to 15, each once
Outputs:
- attended: bfloat16 [2048, 8192], P('ctx', 'head')
- probe_out: bfloat16 [2048, 8192], P('ctx', 'head')
- probe_norm: float32 [], replicated
Inputs may be any that keep to these rules, and one draw needn't show every extreme that they name: `block_order`: each block index appears exactly once.
All inputs are finite; a program needn't handle non-finite values.
Results may differ from a plain program's by a relative error of at most 0.025.
Values may be sent and summed in bfloat16 or wider, within the bound.
A program may use at most 64 MiB of HBM per device.

v0:
```python
import math

import jax
import jax.numpy as jnp
from jax import lax
from jax.sharding import PartitionSpec as P

HEAD_DIM = 128


floor_score = -1e30


def lookup(table, entries):
    return jnp.sum(jnp.where(entries[..., None] == jnp.arange(table.shape[0]), table, 0), axis=-1)


def attend(
    query_block, qtan_block, key_block, value_block, ktan_block, vtan_block, visible, running
):
    factor = 1.0 / math.sqrt(query_block.shape[-1])
    scores = (
        jnp.einsum("tghd,sgd->tghs", query_block, key_block, preferred_element_type=jnp.float32)
        * factor
    )
    scores = jnp.where(visible[:, None, None, :], scores, floor_score)
    top_old, totals_old, drifts_old, numer_old, tangent_old = running
    top_new = jnp.maximum(top_old, jnp.max(scores, axis=-1))
    shrink = jnp.exp(top_old - top_new)
    weights = jnp.exp(scores - top_new[..., None])
    weights = jnp.where(visible[:, None, None, :], weights, 0.0)
    slopes = (
        jnp.einsum("tghd,sgd->tghs", qtan_block, key_block, preferred_element_type=jnp.float32)
        + jnp.einsum("tghd,sgd->tghs", query_block, ktan_block, preferred_element_type=jnp.float32)
    ) * factor
    tilted = weights * slopes
    totals = shrink * totals_old + jnp.sum(weights, axis=-1)
    drifts = shrink * drifts_old + jnp.sum(tilted, axis=-1)
    low_weights = weights.astype(jnp.bfloat16)
    low_tilted = tilted.astype(jnp.bfloat16)
    numerator = shrink[..., None] * numer_old + jnp.einsum(
        "tghs,sgd->tghd", low_weights, value_block, preferred_element_type=jnp.float32
    )
    tangent_num = (
        shrink[..., None] * tangent_old
        + jnp.einsum("tghs,sgd->tghd", low_tilted, value_block, preferred_element_type=jnp.float32)
        + jnp.einsum("tghs,sgd->tghd", low_weights, vtan_block, preferred_element_type=jnp.float32)
    )
    return (top_new, totals, drifts, numerator, tangent_num)


def empty_sums(q_four):
    stat_shape = q_four.shape[:3]
    return (
        jnp.full(stat_shape, floor_score, jnp.float32),
        jnp.zeros(stat_shape, jnp.float32),
        jnp.zeros(stat_shape, jnp.float32),
        jnp.zeros(q_four.shape, jnp.float32),
        jnp.zeros(q_four.shape, jnp.float32),
    )


def make_fold(q_four, dq_four, query_pos, block_order, block_rows):

    def fold_keys(running, pieces, start):
        length = pieces[0].shape[0]
        span = 512

        def sweep(sweep_no, held):
            offset = sweep_no * span
            k_part = lax.dynamic_slice_in_dim(pieces[0], offset, span, 0)
            v_part = lax.dynamic_slice_in_dim(pieces[1], offset, span, 0)
            dk_part = lax.dynamic_slice_in_dim(pieces[2], offset, span, 0)
            dv_part = lax.dynamic_slice_in_dim(pieces[3], offset, span, 0)
            key_index = offset + jnp.arange(span, dtype=jnp.int32)
            key_pos = (
                lookup(block_order, key_index // block_rows) * block_rows + key_index % block_rows
            )
            visible = key_pos[None, :] <= query_pos[:, None]
            return attend(q_four, dq_four, k_part, v_part, dk_part, dv_part, visible, held)

        return lax.fori_loop(0, length // span, sweep, running)

    return fold_keys


def finish(final, width):
    top_final, totals, drifts, numerator, tangent_num = final
    rows = numerator.shape[0]
    attended = (numerator / totals[..., None]).astype(jnp.bfloat16).reshape(rows, width)
    probe = (tangent_num - numerator * drifts[..., None] / totals[..., None]) / totals[..., None]
    square_sum = jnp.sum(probe * probe)
    probe_out = probe.astype(jnp.bfloat16).reshape(rows, width)
    return (attended, probe_out, square_sum)


def shards(queries, key_rows, value_rows, query_tangent, key_tangent, value_tangent, block_order):
    row_count = queries.shape[0]
    width = queries.shape[1]
    groups = key_rows.shape[1] // HEAD_DIM
    shares = width // key_rows.shape[1]
    q_four = queries.reshape(row_count, groups, shares, HEAD_DIM)
    dq_four = query_tangent.reshape(row_count, groups, shares, HEAD_DIM)
    k_three = key_rows.reshape(row_count, groups, HEAD_DIM)
    v_three = value_rows.reshape(row_count, groups, HEAD_DIM)
    dk_three = key_tangent.reshape(row_count, groups, HEAD_DIM)
    dv_three = value_tangent.reshape(row_count, groups, HEAD_DIM)
    empty = empty_sums(q_four)
    count = lax.axis_size("ctx")
    own_index = lax.axis_index("ctx")
    own_block = lookup(block_order, own_index)
    local_rows = jnp.arange(row_count, dtype=jnp.int32)
    query_pos = own_block * row_count + local_rows
    fold_keys = make_fold(q_four, dq_four, query_pos, block_order, row_count)
    final = fold_keys(
        empty,
        (
            lax.all_gather(k_three, "ctx", axis=0, tiled=True),
            lax.all_gather(v_three, "ctx", axis=0, tiled=True),
            lax.all_gather(dk_three, "ctx", axis=0, tiled=True),
            lax.all_gather(dv_three, "ctx", axis=0, tiled=True),
        ),
        jnp.int32(0),
    )
    attended, probe_out, square_sum = finish(final, width)
    total_squares = lax.psum(square_sum, ("ctx", "head"))
    entries = row_count * width * count * lax.axis_size("head")
    probe_norm = jnp.sqrt(total_squares / entries)
    return (attended, probe_out, probe_norm)


def solution(mesh):
    in_specs = (
        P("ctx", "head"),
        P("ctx", "head"),
        P("ctx", "head"),
        P("ctx", "head"),
        P("ctx", "head"),
        P("ctx", "head"),
        P(),
    )
    out_specs = (P("ctx", "head"), P("ctx", "head"), P())
    return jax.shard_map(shards, mesh=mesh, in_specs=in_specs, out_specs=out_specs, check_vma=False)
```

profile of v0, /device:TPU:0, one launch (start us, length us, event | category | flops | bytes accessed | tf_op | source)
XLA Modules:
  0.0 332.2 jit_solution(9713154046225608924)
XLA Ops:
  7.2 1.7 copy.35
  20.4 33.7 %all-gather.5.cloned.1.call-done = bf16[2048,4,128]{0,2,1:T(8,128)(2,1)} async-done(((bf16[128,4,128]{0,2,1:T(8,128)(2,1)}), bf16[2048,4,128]{0,2,1:T(8,128)(2,1)}) %all-gather.5.cloned.1.call-update) | async-done | bytes 2097168 | tf_op jit(solution)/shard_map/all_gather | solution.py:118
  54.1 42.3 %all-gather.9.cloned.1.call-done = bf16[2048,4,128]{0,2,1:T(8,128)(2,1)} async-done(((bf16[128,4,128]{0,2,1:T(8,128)(2,1)}), bf16[2048,4,128]{0,2,1:T(8,128)(2,1)}) %all-gather.9.cloned.1.call-update) | async-done | bytes 2097168 | tf_op jit(solution)/shard_map/all_gather | solution.py:119
  96.4 42.3 %all-gather.7.cloned.1.call-done = bf16[2048,4,128]{0,2,1:T(8,128)(2,1)} async-done(((bf16[128,4,128]{0,2,1:T(8,128)(2,1)}), bf16[2048,4,128]{0,2,1:T(8,128)(2,1)}) %all-gather.7.cloned.1.call-update) | async-done | bytes 2097168 | tf_op jit(solution)/shard_map/all_gather | solution.py:120
  138.7 42.2 %all-gather.11.cloned.1.call-done = bf16[2048,4,128]{0,2,1:T(8,128)(2,1)} async-done(((bf16[128,4,128]{0,2,1:T(8,128)(2,1)}), bf16[2048,4,128]{0,2,1:T(8,128)(2,1)}) %all-gather.11.cloned.1.call-update) | async-done | bytes 2097168 | tf_op jit(solution)/shard_map/all_gather | solution.py:121
  180.9 96.9 %while.24 = (s32[]{:T(128)}, f32[128,4,8]{0,2,1:T(8,128)S(1)}, f32[128,4,8]{0,2,1:T(8,128)}, f32[128,4,8]{0,2,1:T(8,128)}, f32[128,4,8,128]{0,3,2,1:T(8,128)}, /...) while((s32[]{:T(128)}, f32[128,4,8]{0,2,1:T(8,128)S(1)}, ...), condition=%wide.region_6.7_spmd.clone, body=%wide.region_1.6_spmd.clone.sunk | while | flops 3281652224 | bytes 129578640 | solution.py:82
  181.1 2.7 fusion.75
  183.9 2.8 fusion.73
  186.7 5.8 %fusion.76 = (f32[128,4,8]{0,2,1:T(8,128)}, bf16[128,4,8,512]{0,3,2,1:T(8,128)(2,1)S(1)}) fusion(f32[4,512,128,8]{2,1,3,0:T(8,128)S(1)} %fusion.75, bf16[128,4,8,128]{3,0,2,1:T(8,128)(2,1)} %get-tuple-element.602, bf16[2048,4,128]{0,2,1:T(8,128)(2,1)} %get-tuple-element.604, s32[]{:T(128)S(6)} %select_n.147, ...), kind=kOutput, calls=%fused_computation.61.clone.1 | convolution fusion | flops 555741184 | bytes 22642692 | tf_op jit(solution)/shard_map/while/body/eval_jaxpr/tghd,sgd->tghs/dot_general | solution.py:34
  192.6 3.0 fusion.74
  195.7 2.6 bitcast_add_fusion.5
  198.4 3.8 %fusion.79 = f32[4,128,128,8]{2,1,3,0:T(8,128)S(1)} fusion(bf16[2048,4,128]{0,2,1:T(8,128)(2,1)} %get-tuple-element.606, s32[]{:T(128)S(6)} %select_n.147, f32[128,4,8]{0,2,1:T(8,128)S(1)} %select_maximum_fusion.2, f32[4,512,128,8]{2,1,3,0:T(8,128)S(1)} %get-tuple-element.553, pred[128,512]{0,1:T(8,128)(4,1)S(1)} %copy-done.3), kind=kOutput, calls=%fused_computation.19.clone.1 | convolution fusion | flops 547356672 | bytes 11091972 | tf_op jit(solution)/shard_map/while/body/eval_jaxpr/tghs,sgd->tghd/dot_general | solution.py:47
  205.4 2.7 fusion.75
  208.1 2.8 fusion.73
  211.0 5.8 %fusion.76 = (f32[128,4,8]{0,2,1:T(8,128)}, bf16[128,4,8,512]{0,3,2,1:T(8,128)(2,1)S(1)}) fusion(f32[4,512,128,8]{2,1,3,0:T(8,128)S(1)} %fusion.75, bf16[128,4,8,128]{3,0,2,1:T(8,128)(2,1)} %get-tuple-element.602, bf16[2048,4,128]{0,2,1:T(8,128)(2,1)} %get-tuple-element.604, s32[]{:T(128)S(6)} %select_n.147, ...), kind=kOutput, calls=%fused_computation.61.clone.1 | convolution fusion | flops 555741184 | bytes 22642692 | tf_op jit(solution)/shard_map/while/body/eval_jaxpr/tghd,sgd->tghs/dot_general | solution.py:34
  216.8 3.0 fusion.74
  219.9 2.6 bitcast_add_fusion.5
  222.6 3.8 %fusion.79 = f32[4,128,128,8]{2,1,3,0:T(8,128)S(1)} fusion(bf16[2048,4,128]{0,2,1:T(8,128)(2,1)} %get-tuple-element.606, s32[]{:T(128)S(6)} %select_n.147, f32[128,4,8]{0,2,1:T(8,128)S(1)} %select_maximum_fusion.2, f32[4,512,128,8]{2,1,3,0:T(8,128)S(1)} %get-tuple-element.553, pred[128,512]{0,1:T(8,128)(4,1)S(1)} %copy-done.3), kind=kOutput, calls=%fused_computation.19.clone.1 | convolution fusion | flops 547356672 | bytes 11091972 | tf_op jit(solution)/shard_map/while/body/eval_jaxpr/tghs,sgd->tghd/dot_general | solution.py:47
  229.6 2.7 fusion.75
  232.3 2.8 fusion.73
  235.2 5.8 %fusion.76 = (f32[128,4,8]{0,2,1:T(8,128)}, bf16[128,4,8,512]{0,3,2,1:T(8,128)(2,1)S(1)}) fusion(f32[4,512,128,8]{2,1,3,0:T(8,128)S(1)} %fusion.75, bf16[128,4,8,128]{3,0,2,1:T(8,128)(2,1)} %get-tuple-element.602, bf16[2048,4,128]{0,2,1:T(8,128)(2,1)} %get-tuple-element.604, s32[]{:T(128)S(6)} %select_n.147, ...), kind=kOutput, calls=%fused_computation.61.clone.1 | convolution fusion | flops 555741184 | bytes 22642692 | tf_op jit(solution)/shard_map/while/body/eval_jaxpr/tghd,sgd->tghs/dot_general | solution.py:34
  241.0 3.0 fusion.74
  244.2 2.6 bitcast_add_fusion.5
  246.9 3.8 %fusion.79 = f32[4,128,128,8]{2,1,3,0:T(8,128)S(1)} fusion(bf16[2048,4,128]{0,2,1:T(8,128)(2,1)} %get-tuple-element.606, s32[]{:T(128)S(6)} %select_n.147, f32[128,4,8]{0,2,1:T(8,128)S(1)} %select_maximum_fusion.2, f32[4,512,128,8]{2,1,3,0:T(8,128)S(1)} %get-tuple-element.553, pred[128,512]{0,1:T(8,128)(4,1)S(1)} %copy-done.3), kind=kOutput, calls=%fused_computation.19.clone.1 | convolution fusion | flops 547356672 | bytes 11091972 | tf_op jit(solution)/shard_map/while/body/eval_jaxpr/tghs,sgd->tghd/dot_general | solution.py:47
  253.8 2.7 fusion.75
  256.5 2.8 fusion.73
  259.4 5.8 %fusion.76 = (f32[128,4,8]{0,2,1:T(8,128)}, bf16[128,4,8,512]{0,3,2,1:T(8,128)(2,1)S(1)}) fusion(f32[4,512,128,8]{2,1,3,0:T(8,128)S(1)} %fusion.75, bf16[128,4,8,128]{3,0,2,1:T(8,128)(2,1)} %get-tuple-element.602, bf16[2048,4,128]{0,2,1:T(8,128)(2,1)} %get-tuple-element.604, s32[]{:T(128)S(6)} %select_n.147, ...), kind=kOutput, calls=%fused_computation.61.clone.1 | convolution fusion | flops 555741184 | bytes 22642692 | tf_op jit(solution)/shard_map/while/body/eval_jaxpr/tghd,sgd->tghs/dot_general | solution.py:34
  265.2 3.0 fusion.74
  268.4 2.6 bitcast_add_fusion.5
  271.1 3.8 %fusion.79 = f32[4,128,128,8]{2,1,3,0:T(8,128)S(1)} fusion(bf16[2048,4,128]{0,2,1:T(8,128)(2,1)} %get-tuple-element.606, s32[]{:T(128)S(6)} %select_n.147, f32[128,4,8]{0,2,1:T(8,128)S(1)} %select_maximum_fusion.2, f32[4,512,128,8]{2,1,3,0:T(8,128)S(1)} %get-tuple-element.553, pred[128,512]{0,1:T(8,128)(4,1)S(1)} %copy-done.3), kind=kOutput, calls=%fused_computation.19.clone.1 | convolution fusion | flops 547356672 | bytes 11091972 | tf_op jit(solution)/shard_map/while/body/eval_jaxpr/tghs,sgd->tghd/dot_general | solution.py:47
  277.8 3.6 %multiply_reduce_fusion = (f32[]{:T(128)}, bf16[128,4,8,128]{0,3,2,1:T(8,128)(2,1)S(1)}, bf16[128,4,8,128]{0,3,2,1:T(8,128)(2,1)S(1)}) fusion(f32[128,4,8,128]{0,3,2,1:T(8,128)} %get-tuple-element.341, f32[128,4,8]{0,2,1:T(8,128)} %get-tuple-element.340, f32[128,4,8,128]{0,3,2,1:T(8,128)} %get-tuple-element.339, f32[128,4,8]{0,2,1:T(8,128)} %get-tuple-element.342), kind=kLoop, calls=%fused_computation.56 | loop fusion | flops 4718591 | bytes 6324228 | tf_op jit(solution)/shard_map/reduce_sum | solution.py:92
  281.3 39.9 %psum.7 = f32[]{:T(128)} all-reduce(f32[]{:T(128)} %get-tuple-element.449), channel_id=1, replica_groups=mesh['ctx'=16,'head'=2] {'ctx','head'}, use_global_device_ids=true, to_apply=%region_8.9 | all-reduce | flops 1 | bytes 8 | tf_op jit(solution)/shard_map/psum | solution.py:126
  (163 shorter events, 26.2 us)
Async XLA Ops:
  7.2 10.0 %copy-start.7 = (bf16[128,4096]{1,0:T(8,128)(2,1)S(1)}, bf16[128,4096]{1,0:T(8,128)(2,1)}, u32[]{:S(2)}) copy-start(bf16[128,4096]{1,0:T(8,128)(2,1)} %param.12) | copy-start | bytes 3145732
  7.2 46.9 %all-gather.5.cloned.1.call-start = ((), (), s32[]{:S(2)}) async-start(), calls=%async_computation | async-start | bytes 2228224 | tf_op jit(solution)/shard_map/all_gather | solution.py:118
  9.0 87.4 %all-gather.9.cloned.1.call-start = ((), (), s32[]{:S(2)}) async-start(), calls=%async_computation.2 | async-start | bytes 2228224 | tf_op jit(solution)/shard_map/all_gather | solution.py:119
  10.7 128.0 %all-gather.7.cloned.1.call-start = ((), (), s32[]{:S(2)}) async-start(), calls=%async_computation.1 | async-start | bytes 2228224 | tf_op jit(solution)/shard_map/all_gather | solution.py:120
  12.5 168.4 %all-gather.11.cloned.1.call-start = ((), (), s32[]{:S(2)}) async-start(), calls=%async_computation.3 | async-start | bytes 2228224 | tf_op jit(solution)/shard_map/all_gather | solution.py:121
  14.3 4.9 %copy-start.13 = (s32[16]{0:T(128)S(1)}, s32[16]{0:T(128)}, u32[]{:S(2)}) copy-start(s32[16]{0:T(128)} %param.15) | copy-start | bytes 196
  192.5 3.1 copy-start.12
  192.5 3.1 copy-start.10
  192.5 3.1 copy-start.3
  192.5 3.2 copy-start.4
  192.6 3.2 copy-start.5
  198.4 3.8 %copy-start.6 = (f32[128,4,8,128]{0,3,2,1:T(8,128)}, f32[128,4,8,128]{0,3,2,1:T(8,128)S(1)}, u32[]{:S(2)}) copy-start(f32[128,4,8,128]{0,3,2,1:T(8,128)S(1)} %bitcast_add_fusion.5) | copy-start | bytes 6291460 | tf_op jit(solution)/shard_map/while
  198.4 3.8 %copy-start = (f32[128,4,8,128]{0,3,2,1:T(8,128)S(1)}, f32[128,4,8,128]{0,3,2,1:T(8,128)}, u32[]{:S(2)}) copy-start(f32[128,4,8,128]{0,3,2,1:T(8,128)} %get-tuple-element.581) | copy-start | bytes 6291460 | tf_op jit(solution)/shard_map/while
  216.8 3.1 copy-start.12
  216.8 3.1 copy-start.10
  216.8 3.1 copy-start.3
  216.8 3.2 copy-start.4
  216.8 3.2 copy-start.5
  222.6 3.8 %copy-start.6 = (f32[128,4,8,128]{0,3,2,1:T(8,128)}, f32[128,4,8,128]{0,3,2,1:T(8,128)S(1)}, u32[]{:S(2)}) copy-start(f32[128,4,8,128]{0,3,2,1:T(8,128)S(1)} %bitcast_add_fusion.5) | copy-start | bytes 6291460 | tf_op jit(solution)/shard_map/while
  222.6 3.8 %copy-start = (f32[128,4,8,128]{0,3,2,1:T(8,128)S(1)}, f32[128,4,8,128]{0,3,2,1:T(8,128)}, u32[]{:S(2)}) copy-start(f32[128,4,8,128]{0,3,2,1:T(8,128)} %get-tuple-element.581) | copy-start | bytes 6291460 | tf_op jit(solution)/shard_map/while
  241.0 3.1 copy-start.10
  241.0 3.1 copy-start.3
  241.0 3.2 copy-start.4
  241.0 3.2 copy-start.5
  246.8 3.8 %copy-start.6 = (f32[128,4,8,128]{0,3,2,1:T(8,128)}, f32[128,4,8,128]{0,3,2,1:T(8,128)S(1)}, u32[]{:S(2)}) copy-start(f32[128,4,8,128]{0,3,2,1:T(8,128)S(1)} %bitcast_add_fusion.5) | copy-start | bytes 6291460 | tf_op jit(solution)/shard_map/while
  246.8 3.8 %copy-start = (f32[128,4,8,128]{0,3,2,1:T(8,128)S(1)}, f32[128,4,8,128]{0,3,2,1:T(8,128)}, u32[]{:S(2)}) copy-start(f32[128,4,8,128]{0,3,2,1:T(8,128)} %get-tuple-element.581) | copy-start | bytes 6291460 | tf_op jit(solution)/shard_map/while
  265.2 3.1 copy-start.10
  265.2 3.1 copy-start.3
  265.2 3.2 copy-start.4
  265.2 3.2 copy-start.5
  271.0 3.8 %copy-start.6 = (f32[128,4,8,128]{0,3,2,1:T(8,128)}, f32[128,4,8,128]{0,3,2,1:T(8,128)S(1)}, u32[]{:S(2)}) copy-start(f32[128,4,8,128]{0,3,2,1:T(8,128)S(1)} %bitcast_add_fusion.5) | copy-start | bytes 6291460 | tf_op jit(solution)/shard_map/while
  271.1 3.8 %copy-start = (f32[128,4,8,128]{0,3,2,1:T(8,128)S(1)}, f32[128,4,8,128]{0,3,2,1:T(8,128)}, u32[]{:S(2)}) copy-start(f32[128,4,8,128]{0,3,2,1:T(8,128)} %get-tuple-element.581) | copy-start | bytes 6291460 | tf_op jit(solution)/shard_map/while
  (22 other events, 56.5 us)
Sparse Core Ops, SparseCore 0:
  10.2 43.8 all-gather.4
  56.2 40.1 all-gather.8
  98.6 40.1 all-gather.6
  140.7 40.1 all-gather.10
where the time goes:
time: 333 us; the launch traced here: 332 us
  waiting for transfers between devices  161 us (48%)
  matrix products  77.2 us (23%)
  blocking collectives  39.9 us (12%)
  local copies, waits for them, and re-layouts  19.8 us (6%)
  other arithmetic  17.5 us (5%)
  between operations  16.3 us (5%)
    all_gather x1, waiting for transfers between devices, shards(): lax.all_gather(dk_three, 'ctx', axis=0, tiled=True)  42.3 us
    all_gather x1, waiting for transfers between devices, shards(): lax.all_gather(v_three, 'ctx', axis=0, tiled=True)  42.3 us
    all_gather x1, waiting for transfers between devices, shards(): lax.all_gather(dv_three, 'ctx', axis=0, tiled=True)  42.2 us
    psum x1, blocking collectives, shards(): total_squares = lax.psum(square_sum, ('ctx', 'head'))  39.9 us
    all_gather x1, waiting for transfers between devices, shards(): lax.all_gather(k_three, 'ctx', axis=0, tiled=True)  33.7 us
    dot_general x4, matrix products, attend(): jnp.einsum('tghd,sgd->tghs', query_block, ktan_block, preferred_element_t...  23.2 us
    dot_general x4, matrix products, attend(): jnp.einsum('tghs,sgd->tghd', low_weights, vtan_block, preferred_element_t...  15 us
    reduce_sum x4, other arithmetic, attend(): totals = shrink * totals_old + jnp.sum(weights, axis=-1)  12.1 us
  transfers between devices with their start and end apart: 4, of which 4 were waited for; matrix products, arithmetic and copies ran while one was open for 3% of the time, Pallas kernels for 0%

commit v1 on v0

v1 whole, which is shorter than its diff:
```python
import functools
import math

import jax
import jax.numpy as jnp
from jax import lax
from jax.experimental import pallas as pl
from jax.experimental.pallas import tpu as pltpu
from jax.sharding import PartitionSpec as P

HEAD_DIM = 128
MESH = pl.DeviceIdType.MESH
FLOOR = -1e30


def dot_t(a, b):
    return lax.dot_general(a, b, (((1,), (1,)), ((), ())), preferred_element_type=jnp.float32)


def dot_n(a, b):
    return jnp.dot(a, b, preferred_element_type=jnp.float32)


def kernel(
    n,
    order_ref, q_hbm, dq_hbm, k_ref, v_ref, dk_ref, dv_ref,
    att_ref, probe_ref, square_ref,
    q_vm, dq_vm, qs, kv, acc, tan, top, tot, dri,
    q_sem, recv, send,
):
    depth = n // 4
    me = lax.axis_index("ctx")
    z, y, c = me // 4, (me // 2) % 2, me % 2
    rows = k_ref.shape[0]
    groups = k_ref.shape[1] // HEAD_DIM
    shares = q_vm.shape[1] // k_ref.shape[1]
    stack = rows * shares
    steps = depth * groups

    def at(zz, yy, cc):
        return {"ctx": (zz * 2 + yy) * 2 + cc}

    copies = [
        pltpu.make_async_copy(q_hbm, q_vm, q_sem.at[0]),
        pltpu.make_async_copy(dq_hbm, dq_vm, q_sem.at[1]),
    ]
    for copy in copies:
        copy.start()

    barrier = pltpu.get_barrier_semaphore()
    has_up, has_down = z < depth - 1, z > 0

    def greet(zz, yy, cc):
        pl.semaphore_signal(barrier, inc=1, device_id=at(zz, yy, cc), device_id_type=MESH)

    greet(z, 1 - y, c)
    greet(z, y, 1 - c)

    @pl.when(has_up)
    def _():
        greet(z + 1, y, c)

    @pl.when(has_down)
    def _():
        greet(z - 1, y, c)

    for g in range(groups):
        cols = slice(g * HEAD_DIM, (g + 1) * HEAD_DIM)
        for part, ref in enumerate((k_ref, dk_ref, v_ref, dv_ref)):
            kv[z, g, y, c, :, part * HEAD_DIM : (part + 1) * HEAD_DIM] = ref[:, cols]

    peers = 2 + jnp.where(has_up, 1, 0) + jnp.where(has_down, 1, 0)
    pl.semaphore_wait(barrier, peers)

    def move(zs, g, yy, cc, lane, target):
        return pltpu.make_async_remote_copy(
            src_ref=kv.at[zs, g, yy, cc],
            dst_ref=kv.at[zs, g, yy, cc],
            send_sem=send.at[zs, g, lane],
            recv_sem=recv.at[zs, g, yy, cc],
            device_id=target,
            device_id_type=MESH,
        )

    def up(zs, g):
        return move(zs, g, y, c, 0, at(z + 1, y, c))

    def down(zs, g):
        return move(zs, g, y, c, 1, at(z - 1, y, c))

    def across(zs, g):
        return move(zs, g, y, c, 2, at(z, 1 - y, c))

    def twin(zs, g):
        return move(zs, g, y, c, 3, at(z, y, 1 - c))

    def twin_across(zs, g):
        return move(zs, g, 1 - y, c, 4, at(z, y, 1 - c))

    def goes_up(zs):
        return jnp.logical_and(has_up, zs <= z)

    def goes_down(zs):
        return jnp.logical_and(has_down, zs >= z)

    def pass_on(zs, g):
        @pl.when(goes_up(zs))
        def _():
            up(zs, g).start()

        @pl.when(goes_down(zs))
        def _():
            down(zs, g).start()

        across(zs, g).start()
        twin(zs, g).start()

    for g in range(groups):
        pass_on(z, g)

    for copy in copies:
        copy.wait()

    def stage(g, carry):
        for h in range(shares):
            cols = pl.ds(pl.multiple_of((g * shares + h) * HEAD_DIM, HEAD_DIM), HEAD_DIM)
            qs[g, h * rows : (h + 1) * rows, 0:HEAD_DIM] = dq_vm[:, cols]
            qs[g, h * rows : (h + 1) * rows, HEAD_DIM:] = q_vm[:, cols]
        return carry

    lax.fori_loop(0, groups, stage, 0)

    reach = jnp.minimum(z, depth - 1 - z)
    far = jnp.where(z < depth - 1 - z, 1, -1)

    def source(i):
        near = ((i + 1) // 2) * jnp.where(i % 2 == 1, 1, -1)
        return z + jnp.where(i <= 2 * reach, near, (i - reach) * far)

    own = order_ref[me]
    factor = 1.0 / math.sqrt(HEAD_DIM)
    sharp = factor * math.log2(math.e)
    part_rows = min(stack, 512)

    def fold(zs, g, first):
        block = kv[zs, g].reshape(4 * rows, 4 * HEAD_DIM)
        orders = [order_ref[zs * 4 + j] for j in range(4)]
        if first:
            lane = lax.broadcasted_iota(jnp.int32, (part_rows, rows), 1)
            row = lax.broadcasted_iota(jnp.int32, (part_rows, rows), 0) % rows + own * rows

        def part(r, carry):
            span = pl.ds(pl.multiple_of(r * part_rows, part_rows), part_rows)
            pair = qs[g, span, :]
            scores = dot_t(pair[:, HEAD_DIM:], block[:, :HEAD_DIM]) * sharp
            slopes = dot_t(pair, block[:, : 2 * HEAD_DIM])
            pieces = []
            for j in range(4):
                piece = scores[:, j * rows : (j + 1) * rows]
                if first:
                    piece = jnp.where(lane + orders[j] * rows <= row, piece, FLOOR)
                else:
                    piece = piece + jnp.where(orders[j] <= own, 0.0, FLOOR)
                pieces.append(piece)
            high = jnp.maximum(
                jnp.maximum(pieces[0], pieces[1]), jnp.maximum(pieces[2], pieces[3])
            )
            high = jnp.broadcast_to(jnp.max(high, axis=1, keepdims=True), high.shape)
            if not first:
                old = top[g, span, :]
                high = jnp.maximum(old, high)
                shrink = jnp.exp2(old - high)
            top[g, span, :] = high
            weights, tilted = [], []
            for j in range(4):
                weights.append(jnp.exp2(pieces[j] - high))
                tilted.append(weights[j] * slopes[:, j * rows : (j + 1) * rows])
            tot_new = (weights[0] + weights[1]) + (weights[2] + weights[3])
            dri_new = (tilted[0] + tilted[1]) + (tilted[2] + tilted[3])
            low_w = jnp.concatenate([w.astype(jnp.bfloat16) for w in weights], axis=1)
            low_t = jnp.concatenate([t.astype(jnp.bfloat16) for t in tilted], axis=1)
            acc_new = dot_n(low_w, block[:, 2 * HEAD_DIM :])
            tan_new = dot_n(low_t, block[:, 2 * HEAD_DIM : 3 * HEAD_DIM])
            if first:
                tot[g, span, :] = tot_new
                dri[g, span, :] = dri_new
                acc[g, span, :] = acc_new
                tan[g, span, :] = tan_new
            else:
                tot[g, span, :] = tot[g, span, :] * shrink + tot_new
                dri[g, span, :] = dri[g, span, :] * shrink + dri_new
                tan[g, span, :] = tan[g, span, :] * shrink + tan_new
                acc[g, span, :] = (
                    acc[g, span, :] * jnp.concatenate([shrink, shrink], axis=1) + acc_new
                )
            return carry

        lax.fori_loop(0, stack // part_rows, part, 0)

    def turn(s, carry):
        @pl.when(jnp.logical_and(s >= groups, s < steps))
        def _():
            zs, g = source(s // groups), s % groups
            twin(zs, g).wait_recv()
            pass_on(zs, g)

        @pl.when(jnp.logical_and(s >= 1, s < steps + 1))
        def _():
            zs, g = source((s - 1) // groups), (s - 1) % groups
            twin_across(zs, g).wait_recv()
            twin_across(zs, g).start()

        def ready(zs, g):
            move(zs, g, y, 1 - c, 0, at(z, y, 1 - c)).wait_recv()
            move(zs, g, 1 - y, 1 - c, 0, at(z, y, 1 - c)).wait_recv()

        @pl.when(jnp.logical_and(s >= 2, s < groups + 2))
        def _():
            g = s - 2
            ready(z, g)
            fold(z, g, True)

        @pl.when(s >= groups + 2)
        def _():
            zs, g = source((s - 2) // groups), (s - 2) % groups
            ready(zs, g)
            fold(zs, g, False)

        return carry

    lax.fori_loop(0, steps + 2, turn, 0)

    def finish(g, squares):
        for h in range(shares):
            span = slice(h * rows, (h + 1) * rows)
            cols = pl.ds(pl.multiple_of((g * shares + h) * HEAD_DIM, HEAD_DIM), HEAD_DIM)
            inverse = 1.0 / jnp.sum(tot[g, span, :], axis=1, keepdims=True)
            drift = jnp.sum(dri[g, span, :], axis=1, keepdims=True) * factor
            numer = acc[g, span, :HEAD_DIM] * inverse
            tangent = (tan[g, span, :] * factor + acc[g, span, HEAD_DIM:]) * inverse
            probe = tangent - numer * (drift * inverse)
            att_ref[:, cols] = numer.astype(jnp.bfloat16)
            probe_ref[:, cols] = probe.astype(jnp.bfloat16)
            squares = squares + jnp.sum((probe * probe).reshape(rows // 8, 8, HEAD_DIM), axis=0)
        return squares

    square_ref[...] = lax.fori_loop(
        0, groups, finish, jnp.zeros((8, HEAD_DIM), jnp.float32)
    )

    def settle(s, carry):
        zs, g = s // groups, s % groups

        @pl.when(goes_up(zs))
        def _():
            up(zs, g).wait_send()

        @pl.when(goes_down(zs))
        def _():
            down(zs, g).wait_send()

        across(zs, g).wait_send()
        twin(zs, g).wait_send()
        twin_across(zs, g).wait_send()
        return carry

    lax.fori_loop(0, steps, settle, 0)


def shards(n, heads, queries, key_rows, value_rows, query_tangent, key_tangent, value_tangent, block_order):
    rows, width = queries.shape
    groups = key_rows.shape[1] // HEAD_DIM
    stack = rows * width // key_rows.shape[1]
    depth = n // 4
    vmem = pl.BlockSpec(memory_space=pltpu.VMEM)
    hbm = pl.BlockSpec(memory_space=pl.ANY)
    f32, bf16 = jnp.float32, jnp.bfloat16
    attended, probe_out, squares = pl.pallas_call(
        functools.partial(kernel, n),
        out_shape=(
            jax.ShapeDtypeStruct((rows, width), bf16),
            jax.ShapeDtypeStruct((rows, width), bf16),
            jax.ShapeDtypeStruct((8, HEAD_DIM), f32),
        ),
        in_specs=[pl.BlockSpec(memory_space=pltpu.SMEM), hbm, hbm, vmem, vmem, vmem, vmem],
        out_specs=(vmem, vmem, vmem),
        scratch_shapes=[
            pltpu.VMEM((rows, width), bf16),
            pltpu.VMEM((rows, width), bf16),
            pltpu.VMEM((groups, stack, 2 * HEAD_DIM), bf16),
            pltpu.VMEM((depth, groups, 2, 2, rows, 4 * HEAD_DIM), bf16),
            pltpu.VMEM((groups, stack, 2 * HEAD_DIM), f32),
            pltpu.VMEM((groups, stack, HEAD_DIM), f32),
            pltpu.VMEM((groups, stack, HEAD_DIM), f32),
            pltpu.VMEM((groups, stack, HEAD_DIM), f32),
            pltpu.VMEM((groups, stack, HEAD_DIM), f32),
            pltpu.SemaphoreType.DMA((2,)),
            pltpu.SemaphoreType.DMA((depth, groups, 2, 2)),
            pltpu.SemaphoreType.DMA((depth, groups, 5)),
        ],
        compiler_params=pltpu.CompilerParams(
            collective_id=0, has_side_effects=True, vmem_limit_bytes=56 * 2**20
        ),
    )(block_order, queries, query_tangent, key_rows, value_rows, key_tangent, value_tangent)
    total_squares = lax.psum(jnp.sum(squares), ("ctx", "head"))
    entries = rows * width * n * heads
    return attended, probe_out, jnp.sqrt(total_squares / entries)


def solution(mesh):
    split = P("ctx", "head")
    return jax.shard_map(
        functools.partial(shards, mesh.shape["ctx"], mesh.shape["head"]),
        mesh=mesh,
        in_specs=(split,) * 6 + (P(),),
        out_specs=(split, split, P()),
        check_vma=False,
    )
```

time: 333 us -> 116 us (0.35)
  waiting for transfers between devices: 161 us -> 0 us
  matrix products: 77.2 us -> 0 us
  Pallas kernels: 0 us -> 70.7 us
  local copies, waits for them, and re-layouts: 19.8 us -> 3.35 us
  other arithmetic: 17.5 us -> 1.29 us
  between operations: 16.3 us -> 2.47 us
    all_gather x4 -> x0, waiting for transfers between devices: 160 us -> none  [the longest x1 42.3 us: shards(): lax.all_gather(dk_three, 'ctx', axis=0, tiled=True)]
    dot_general x24 -> x0, matrix products: 77.2 us -> none  [the longest x4 23.2 us: attend(): jnp.einsum('tghd,sgd->tghs', query_block, ktan_block, preferred_element_t...]
    pallas_call x0 -> x1, Pallas kernels: none -> 70.7 us  [shards(): pl.pallas_call(functools.partial(kernel, n), out_shape=(jax.ShapeDtypeStr...]
    reduce_sum x10 -> x1, other arithmetic: 16.7 us -> 1.29 us  [shards(): total_squares = lax.psum(jnp.sum(squares), ('ctx', 'head'))]
    unnamed x12 -> x4, local copies, waits for them, and re-layouts: 11.6 us -> 3.35 us
    while x100 -> x0, local copies, waits for them, and re-layouts: 5.5 us -> none
  transfers between devices with their start and end apart: 4 -> 0, of which waited for: 4 -> 0; matrix products, arithmetic and copies ran while one was open for 3% -> 0% of each run, Pallas kernels for 0% -> 0%
where the time goes in v1:
time: 116 us
  Pallas kernels  70.7 us (61%)
  blocking collectives  38 us (33%)
  local copies, waits for them, and re-layouts  3.35 us (3%)
  between operations  2.47 us (2%)
  other arithmetic  1.29 us (1%)
    pallas_call x1, Pallas kernels, shards(): pl.pallas_call(functools.partial(kernel, n), out_shape=(jax.ShapeDtypeStr...  70.7 us
    psum x1, blocking collectives, shards(): total_squares = lax.psum(jnp.sum(squares), ('ctx', 'head'))  38 us
    unnamed x4, local copies, waits for them, and re-layouts  3.35 us

profile of v1, /device:TPU:0, one launch (start us, length us, event | category | flops | bytes accessed | tf_op | source)
XLA Modules:
  0.0 115.8 jit_solution(15496286369729093977)
XLA Ops:
  0.6 70.7 %shard_map.94 = (bf16[128,4096]{1,0:T(8,128)(2,1)}, bf16[128,4096]{1,0:T(8,128)(2,1)}, f32[8,128]{1,0:T(8,128)}) custom-call(s32[16]{0:T(128)} %order_ref.1, bf16[128,4096]{1,0:T(8,128)(2,1)} %q_hbm.1, bf16[128,4096]{1,0:T(8,128)(2,1)} %dq_hbm.1, bf16[128,512]{1,0:T(8,128)(2,1)} %k_ref.1, bf16[128,512]{1,0:T(8,128)(2,1)} %v_ref.1, bf16[128,512]{1,0:T(8,128)(2,1)} %dk_ref.1, ...), custom_call_target="tpu_custom_call" | custom-call | tf_op jit(solution)/shard_map/pallas_call | solution.py:278
  71.4 1.3 %reduce_sum.9 = f32[]{:T(128)} reduce(f32[8,128]{1,0:T(8,128)} %get-tuple-element.8, f32[]{:T(128)} %constant.1.clone.1), dimensions={0,1}, to_apply=%region_0.0 | reduce | flops 1023 | bytes 4104 | tf_op jit(solution)/shard_map/reduce_sum | solution.py:305
  72.7 38.0 %psum.7 = f32[]{:T(128)} all-reduce(f32[]{:T(128)} %reduce_sum.9), channel_id=1, replica_groups=mesh['ctx'=16,'head'=2] {'ctx','head'}, use_global_device_ids=true, to_apply=%region_1.0 | all-reduce | flops 1 | bytes 8 | tf_op jit(solution)/shard_map/psum | solution.py:305
  111.4 0.0 copy-start
  111.4 2.4 %copy.12 = bf16[128,4096]{1,0:T(8,128)(2,1)} copy(bf16[128,4096]{1,0:T(8,128)(2,1)} %get-tuple-element.12) | data formatting | bytes 2097152
  113.7 0.0 copy-done
  113.7 1.0 copy.13
Async XLA Ops:
  111.4 2.4 %copy-start = (bf16[128,4096]{1,0:T(8,128)(2,1)S(1)}, bf16[128,4096]{1,0:T(8,128)(2,1)}, u32[]{:S(2)}) copy-start(bf16[128,4096]{1,0:T(8,128)(2,1)} %get-tuple-element.13) | copy-start | bytes 3145732

commit v2 on v1

--- a/solution.py
+++ b/solution.py
@@ -23,10 +23,12 @@
 
 def kernel(
     n,
+    heads,
     order_ref, q_hbm, dq_hbm, k_ref, v_ref, dk_ref, dv_ref,
-    att_ref, probe_ref, square_ref,
+    att_ref, probe_ref, norm_ref,
     q_vm, dq_vm, qs, kv, acc, tan, top, tot, dri,
-    q_sem, recv, send,
+    plane_box, line_box, head_box,
+    q_sem, recv, send, plane_sem, line_sem, head_sem,
 ):
     depth = n // 4
     me = lax.axis_index("ctx")
@@ -50,27 +52,23 @@
     barrier = pltpu.get_barrier_semaphore()
     has_up, has_down = z < depth - 1, z > 0
 
-    def greet(zz, yy, cc):
-        pl.semaphore_signal(barrier, inc=1, device_id=at(zz, yy, cc), device_id_type=MESH)
-
-    greet(z, 1 - y, c)
-    greet(z, y, 1 - c)
-
-    @pl.when(has_up)
-    def _():
-        greet(z + 1, y, c)
-
-    @pl.when(has_down)
-    def _():
-        greet(z - 1, y, c)
+    head = lax.axis_index("head")
+    spot = y * 2 + c
+    plane = (4, spot, lambda i: {"ctx": z * 4 + i})
+    line = (depth, z, lambda i: {"ctx": i * 4 + spot})
+    across_heads = (heads, head, lambda i: {"head": i})
+    for count, mine, device in (plane, line, across_heads):
+        for step in range(1, count):
+            pl.semaphore_signal(
+                barrier, inc=1, device_id=device((mine + step) % count), device_id_type=MESH
+            )
 
     for g in range(groups):
         cols = slice(g * HEAD_DIM, (g + 1) * HEAD_DIM)
         for part, ref in enumerate((k_ref, dk_ref, v_ref, dv_ref)):
             kv[z, g, y, c, :, part * HEAD_DIM : (part + 1) * HEAD_DIM] = ref[:, cols]
 
-    peers = 2 + jnp.where(has_up, 1, 0) + jnp.where(has_down, 1, 0)
-    pl.semaphore_wait(barrier, peers)
+    pl.semaphore_wait(barrier, 3 + (depth - 1) + (heads - 1))
 
     def move(zs, g, yy, cc, lane, target):
         return pltpu.make_async_remote_copy(
@@ -140,7 +138,7 @@
     own = order_ref[me]
     factor = 1.0 / math.sqrt(HEAD_DIM)
     sharp = factor * math.log2(math.e)
-    part_rows = min(stack, 512)
+    part_rows = min(stack, 1024)
 
     def fold(zs, g, first):
         block = kv[zs, g].reshape(4 * rows, 4 * HEAD_DIM)
@@ -244,9 +242,37 @@
             squares = squares + jnp.sum((probe * probe).reshape(rows // 8, 8, HEAD_DIM), axis=0)
         return squares
 
-    square_ref[...] = lax.fori_loop(
-        0, groups, finish, jnp.zeros((8, HEAD_DIM), jnp.float32)
-    )
+    squares = lax.fori_loop(0, groups, finish, jnp.zeros((8, HEAD_DIM), jnp.float32))
+
+    def add_up(value, box, sem, partners):
+        count, mine, device = partners
+        box[mine] = value
+
+        def pass_to(step, slot):
+            return pltpu.make_async_remote_copy(
+                src_ref=box.at[mine],
+                dst_ref=box.at[slot],
+                send_sem=sem.at[0, step],
+                recv_sem=sem.at[1, slot],
+                device_id=device((mine + step) % count),
+                device_id_type=MESH,
+            )
+
+        for step in range(1, count):
+            pass_to(step, mine).start()
+        for step in range(1, count):
+            pass_to(step, (mine + step) % count).wait_recv()
+        for step in range(1, count):
+            pass_to(step, mine).wait_send()
+        return jnp.sum(box[...], axis=0)
+
+    squares = add_up(squares, plane_box, plane_sem, plane)
+    squares = add_up(squares, line_box, line_sem, line)
+    if heads > 1:
+        squares = add_up(squares, head_box, head_sem, across_heads)
+    entries = rows * q_vm.shape[1] * n * heads
+    total = jnp.sum(jnp.sum(squares, axis=0, keepdims=True), axis=1, keepdims=True)
+    norm_ref[...] = jnp.sqrt(total / entries)
 
     def settle(s, carry):
         zs, g = s // groups, s % groups
@@ -275,12 +301,12 @@
     vmem = pl.BlockSpec(memory_space=pltpu.VMEM)
     hbm = pl.BlockSpec(memory_space=pl.ANY)
     f32, bf16 = jnp.float32, jnp.bfloat16
-    attended, probe_out, squares = pl.pallas_call(
-        functools.partial(kernel, n),
+    attended, probe_out, norm = pl.pallas_call(
+        functools.partial(kernel, n, heads),
         out_shape=(
             jax.ShapeDtypeStruct((rows, width), bf16),
             jax.ShapeDtypeStruct((rows, width), bf16),
-            jax.ShapeDtypeStruct((8, HEAD_DIM), f32),
+            jax.ShapeDtypeStruct((1, 1), f32),
         ),
         in_specs=[pl.BlockSpec(memory_space=pltpu.SMEM), hbm, hbm, vmem, vmem, vmem, vmem],
         out_specs=(vmem, vmem, vmem),
@@ -294,17 +320,21 @@
             pltpu.VMEM((groups, stack, HEAD_DIM), f32),
             pltpu.VMEM((groups, stack, HEAD_DIM), f32),
             pltpu.VMEM((groups, stack, HEAD_DIM), f32),
+            pltpu.VMEM((4, 8, HEAD_DIM), f32),
+            pltpu.VMEM((depth, 8, HEAD_DIM), f32),
+            pltpu.VMEM((heads, 8, HEAD_DIM), f32),
             pltpu.SemaphoreType.DMA((2,)),
             pltpu.SemaphoreType.DMA((depth, groups, 2, 2)),
             pltpu.SemaphoreType.DMA((depth, groups, 5)),
+            pltpu.SemaphoreType.DMA((2, 4)),
+            pltpu.SemaphoreType.DMA((2, depth)),
+            pltpu.SemaphoreType.DMA((2, heads)),
         ],
         compiler_params=pltpu.CompilerParams(
             collective_id=0, has_side_effects=True, vmem_limit_bytes=56 * 2**20
         ),
     )(block_order, queries, query_tangent, key_rows, value_rows, key_tangent, value_tangent)
-    total_squares = lax.psum(jnp.sum(squares), ("ctx", "head"))
-    entries = rows * width * n * heads
-    return attended, probe_out, jnp.sqrt(total_squares / entries)
+    return attended, probe_out, norm.reshape(())
 
 
 def solution(mesh):

time: 116 us -> 85.1 us (0.73)
  blocking collectives: 38 us -> 0 us
  Pallas kernels: 70.7 us -> 79.1 us
  other arithmetic: 1.29 us -> 0 us
    psum x1 -> x0, blocking collectives: 38 us -> none  [shards(): total_squares = lax.psum(jnp.sum(squares), ('ctx', 'head'))]
    pallas_call x1, Pallas kernels: 70.7 us -> 79.1 us  [shards(): pl.pallas_call(functools.partial(kernel, n, heads), out_shape=(jax.ShapeD...]
    reduce_sum x1 -> x0, other arithmetic: 1.29 us -> none  [shards(): total_squares = lax.psum(jnp.sum(squares), ('ctx', 'head'))]
where the time goes in v2:
time: 85.1 us; the launch traced here: 84.9 us
  Pallas kernels  79.1 us (93%)
  local copies, waits for them, and re-layouts  3.35 us (4%)
  between operations  2.4 us (3%)
    pallas_call x1, Pallas kernels, shards(): pl.pallas_call(functools.partial(kernel, n, heads), out_shape=(jax.ShapeD...  79.1 us
    unnamed x4, local copies, waits for them, and re-layouts  3.35 us

profile of v2, /device:TPU:0, one launch (start us, length us, event | category | flops | bytes accessed | tf_op | source)
XLA Modules:
  0.0 84.9 jit_solution(2158396256325197386)
XLA Ops:
  0.6 79.1 %shard_map.94 = (bf16[128,4096]{1,0:T(8,128)(2,1)}, bf16[128,4096]{1,0:T(8,128)(2,1)}, f32[1,1]{1,0:T(1,128)}) custom-call(s32[16]{0:T(128)} %order_ref.1, bf16[128,4096]{1,0:T(8,128)(2,1)} %q_hbm.1, bf16[128,4096]{1,0:T(8,128)(2,1)} %dq_hbm.1, bf16[128,512]{1,0:T(8,128)(2,1)} %k_ref.1, bf16[128,512]{1,0:T(8,128)(2,1)} %v_ref.1, bf16[128,512]{1,0:T(8,128)(2,1)} %dk_ref.1, ...), custom_call_target="tpu_custom_call" | custom-call | tf_op jit(solution)/shard_map/pallas_call | solution.py:304
  79.8 0.0 copy-start
  79.8 2.4 %copy.13 = bf16[128,4096]{1,0:T(8,128)(2,1)} copy(bf16[128,4096]{1,0:T(8,128)(2,1)} %get-tuple-element.12) | data formatting | bytes 2097152
  82.2 0.0 copy-done
  82.2 1.0 %copy.14 = bf16[128,4096]{1,0:T(8,128)(2,1)} copy(bf16[128,4096]{1,0:T(8,128)(2,1)S(1)} %copy-done) | data formatting | bytes 2097152
Async XLA Ops:
  79.8 2.4 %copy-start = (bf16[128,4096]{1,0:T(8,128)(2,1)S(1)}, bf16[128,4096]{1,0:T(8,128)(2,1)}, u32[]{:S(2)}) copy-start(bf16[128,4096]{1,0:T(8,128)(2,1)} %get-tuple-element.13) | copy-start | bytes 3145732

commit v3 on v2

--- a/solution.py
+++ b/solution.py
@@ -202,9 +202,9 @@
             twin(zs, g).wait_recv()
             pass_on(zs, g)
 
-        @pl.when(jnp.logical_and(s >= 1, s < steps + 1))
-        def _():
-            zs, g = source((s - 1) // groups), (s - 1) % groups
+        @pl.when(jnp.logical_and(s >= 2, s < steps + 2))
+        def _():
+            zs, g = source((s - 2) // groups), (s - 2) % groups
             twin_across(zs, g).wait_recv()
             twin_across(zs, g).start()
 
@@ -212,21 +212,21 @@
             move(zs, g, y, 1 - c, 0, at(z, y, 1 - c)).wait_recv()
             move(zs, g, 1 - y, 1 - c, 0, at(z, y, 1 - c)).wait_recv()
 
-        @pl.when(jnp.logical_and(s >= 2, s < groups + 2))
-        def _():
-            g = s - 2
+        @pl.when(jnp.logical_and(s >= 3, s < groups + 3))
+        def _():
+            g = s - 3
             ready(z, g)
             fold(z, g, True)
 
-        @pl.when(s >= groups + 2)
-        def _():
-            zs, g = source((s - 2) // groups), (s - 2) % groups
+        @pl.when(s >= groups + 3)
+        def _():
+            zs, g = source((s - 3) // groups), (s - 3) % groups
             ready(zs, g)
             fold(zs, g, False)
 
         return carry
 
-    lax.fori_loop(0, steps + 2, turn, 0)
+    lax.fori_loop(0, steps + 3, turn, 0)
 
     def finish(g, squares):
         for h in range(shares):

time: 85.1 us -> 78.5 us (0.922)
  Pallas kernels: 79.1 us -> 72.6 us
    pallas_call x1, Pallas kernels: 79.1 us -> 72.6 us  [shards(): pl.pallas_call(functools.partial(kernel, n, heads), out_shape=(jax.ShapeD...]
where the time goes in v3:
time: 78.5 us; the launch traced here: 78.3 us
  Pallas kernels  72.6 us (92%)
  local copies, waits for them, and re-layouts  3.35 us (4%)
  between operations  2.4 us (3%)
    pallas_call x1, Pallas kernels, shards(): pl.pallas_call(functools.partial(kernel, n, heads), out_shape=(jax.ShapeD...  72.6 us
    unnamed x4, local copies, waits for them, and re-layouts  3.35 us

profile of v3, /device:TPU:0, one launch (start us, length us, event | category | flops | bytes accessed | tf_op | source)
XLA Modules:
  0.0 78.3 jit_solution(10234827570496950688)
XLA Ops:
  0.6 72.6 %shard_map.94 = (bf16[128,4096]{1,0:T(8,128)(2,1)}, bf16[128,4096]{1,0:T(8,128)(2,1)}, f32[1,1]{1,0:T(1,128)}) custom-call(s32[16]{0:T(128)} %order_ref.1, bf16[128,4096]{1,0:T(8,128)(2,1)} %q_hbm.1, bf16[128,4096]{1,0:T(8,128)(2,1)} %dq_hbm.1, bf16[128,512]{1,0:T(8,128)(2,1)} %k_ref.1, bf16[128,512]{1,0:T(8,128)(2,1)} %v_ref.1, bf16[128,512]{1,0:T(8,128)(2,1)} %dk_ref.1, ...), custom_call_target="tpu_custom_call" | custom-call | tf_op jit(solution)/shard_map/pallas_call | solution.py:304
  73.2 0.0 copy-start
  73.2 2.4 %copy.13 = bf16[128,4096]{1,0:T(8,128)(2,1)} copy(bf16[128,4096]{1,0:T(8,128)(2,1)} %get-tuple-element.12) | data formatting | bytes 2097152
  75.6 0.0 copy-done
  75.6 1.0 %copy.14 = bf16[128,4096]{1,0:T(8,128)(2,1)} copy(bf16[128,4096]{1,0:T(8,128)(2,1)S(1)} %copy-done) | data formatting | bytes 2097152
Async XLA Ops:
  73.2 2.4 %copy-start = (bf16[128,4096]{1,0:T(8,128)(2,1)S(1)}, bf16[128,4096]{1,0:T(8,128)(2,1)}, u32[]{:S(2)}) copy-start(bf16[128,4096]{1,0:T(8,128)(2,1)} %get-tuple-element.13) | copy-start | bytes 3145732
